TPU v7x, 256 devices: a whole 4x4x8 slice. The times are simulated.
256 devices in a mesh: front: 2 (over y_lo), row: 8 (over y_hi, x), col: 16 (over z, core).
Axes of the slice: x: 4, y: 4 (y_hi: 2, y_lo: 2; y = y_hi * 2 + y_lo), z: 8, core: 2. Of those that a mesh axis runs over, the one named last changes fastest.
Arguments:
- front_orig: bfloat16 [2, 12288, 12288], P('front', 'row', 'col'), as said below
- child_update: bfloat16 [8192, 32768], P(('front', 'row'), 'col'), as said below
- tile_map: int32 [2, 2, 64], replicated, may hold values from 0 to 95, as said below
Outputs:
- update: float32 [2, 12288, 12288], P('front', 'row', 'col')
- factor: float32 [2, 12288, 512], P('front', 'row')
Inputs may be any that keep to these rules, and one draw needn't show every extreme that they name: For every f and c, tile_map[f, c] is one-to-one. tile_map[f, c, i] mod 16 depends only on i mod 16 and takes each of its 16 values once over 16 consecutive i; tile_map[f, c, i] mod 8 depends only on i mod 8. `front_orig`: each front is symmetric in logical order. `child_update`: each child's 8192 x 8192 matrix is symmetric.
All inputs are finite; a program needn't handle non-finite values.
Results may differ from a plain program's by a relative error of at most 0.0009.
Values may be sent and summed in bfloat16 or wider, within the bound.
No kernel may reach another device: no remote copies, remote signals or barrier semaphores. Data moves between devices by JAX's collectives and lax.ppermute only.
A program may use at most 128 MiB of HBM per device.

v0:
```python
import jax
import jax.numpy as jnp
from jax import lax
from jax.sharding import PartitionSpec as P

TILE = 128
PANELS = 2
PANEL = 256
NT = 96
NCT = 64


def from_partner(block, axis, apart):
    count = lax.axis_size(axis)
    route = []
    for low in range(count):
        high = low | 1 << apart
        if high != low and high < count:
            route += [(low, high), (high, low)]
    return lax.ppermute(block, axis, route)


def broadcast(block, axis, holder):
    block = jnp.where(lax.axis_index(axis) == holder, block, jnp.zeros_like(block))
    return lax.psum(block, axis)


def dot_high(left_mat, right_mat):
    return lax.dot_general(
        left_mat,
        right_mat,
        (((1,), (1,)), ((), ())),
        precision=lax.Precision.HIGHEST,
        preferred_element_type=jnp.float32,
    )


def per_device(front_orig, child_update, tile_map):
    row_count = lax.axis_size("row")
    col_count = lax.axis_size("col")
    front_id = lax.axis_index("front")
    row_id = lax.axis_index("row")
    col_id = lax.axis_index("col")
    local_rt = NT // row_count
    local_ct = NT // col_count
    band_rows = NCT // (2 * row_count)
    band_cols = 4 * NCT // col_count
    cap_rows = max(1, band_rows // row_count)
    cap_cols = max(1, band_cols // col_count)
    capacity = cap_rows * cap_cols
    half_cols = col_count // 2
    quarter = col_count // 4
    peer_count = row_count * col_count
    tile_stack = (
        child_update.reshape(band_rows, TILE, band_cols, TILE)
        .transpose(0, 2, 1, 3)
        .reshape(band_rows * band_cols, TILE, TILE)
    )
    along_rows = jnp.arange(band_rows)[:, None]
    along_cols = jnp.arange(band_cols)[None, :]
    child_no = col_id // quarter
    sender_map = tile_map[child_no // 2, child_no % 2]
    mapped_rows = sender_map[(front_id * row_count + row_id) * band_rows + along_rows]
    mapped_cols = sender_map[col_id % quarter * band_cols + along_cols]
    destination = mapped_rows % row_count * col_count + mapped_cols % col_count
    slot_no = along_rows // row_count * cap_cols + along_cols // col_count
    placement = (destination * capacity + slot_no).reshape(-1)
    outgoing = (
        jnp.zeros((peer_count * capacity, TILE, TILE), jnp.bfloat16).at[placement].set(tile_stack)
    )
    arrived = lax.all_to_all(outgoing, ("row", "col"), split_axis=0, concat_axis=0, tiled=True)
    arrived = arrived.reshape(row_count, 2, half_cols, capacity, TILE, TILE)
    kept = lax.dynamic_index_in_dim(arrived, front_id, 1, keepdims=False)
    leaving = lax.dynamic_index_in_dim(arrived, 1 - front_id, 1, keepdims=False)
    incoming = from_partner(leaving, "front", 0)
    slot_count = 2 * row_count * half_cols * capacity
    received = jnp.stack([kept, incoming]).reshape(slot_count, TILE, TILE)
    own_maps = lax.dynamic_index_in_dim(tile_map, front_id, 0, keepdims=False)
    source_side = jnp.arange(2)[:, None, None, None, None]
    source_row = jnp.arange(row_count)[None, :, None, None, None]
    source_col = jnp.arange(half_cols)[None, None, :, None, None]
    tile_row = jnp.arange(band_rows)[None, None, None, :, None]
    tile_col = jnp.arange(band_cols)[None, None, None, None, :]
    source_front = jnp.where(source_side == 0, front_id, 1 - front_id)
    sibling = source_col // quarter
    got_rows = own_maps[sibling, (source_front * row_count + source_row) * band_rows + tile_row]
    got_cols = own_maps[sibling, source_col % quarter * band_cols + tile_col]
    is_mine = (got_rows % row_count == row_id) & (got_cols % col_count == col_id)
    position = (
        ((source_side * row_count + source_row) * half_cols + source_col) * capacity
        + tile_row // row_count * cap_cols
        + tile_col // col_count
    )
    target = got_rows // row_count * local_ct + got_cols // col_count
    spare_tile = local_rt * local_ct
    position = jnp.where(is_mine, position, slot_count)
    slot_table = (
        jnp.full((slot_count,), spare_tile, jnp.int32)
        .at[position.reshape(-1)]
        .set(target.reshape(-1), mode="drop")
    )
    tile_sums = (
        front_orig[0]
        .astype(jnp.float32)
        .reshape(local_rt, TILE, local_ct, TILE)
        .transpose(0, 2, 1, 3)
        .reshape(spare_tile, TILE, TILE)
    )
    tile_sums = jnp.concatenate([tile_sums, jnp.zeros((1, TILE, TILE), jnp.float32)])
    tile_sums = tile_sums.at[slot_table].add(received.astype(jnp.float32))
    front_mat = (
        tile_sums[:spare_tile]
        .reshape(local_rt, local_ct, TILE, TILE)
        .transpose(0, 2, 1, 3)
        .reshape(local_rt * TILE, local_ct * TILE)
    )
    row_tiles = jnp.repeat(row_id + row_count * jnp.arange(local_rt), TILE)
    ratio = col_count // row_count
    offset = (col_id - row_id) // row_count % ratio
    identity = jnp.eye(PANEL, dtype=jnp.float32)
    columns = []
    for panel_no in range(PANELS):
        halves = []
        for side_no in range(2):
            halves.append(broadcast(front_mat[:, :TILE], "col", 2 * panel_no + side_no))
        strip_cols = jnp.concatenate(halves, axis=1)
        block_rows = []
        for side_no in range(2):
            tile_no = 2 * panel_no + side_no
            local_no = tile_no // row_count
            rows_here = strip_cols[local_no * TILE : (local_no + 1) * TILE]
            block_rows.append(jnp.where(row_id == tile_no % row_count, rows_here, 0.0))
        diagonal = lax.psum(jnp.concatenate(block_rows, axis=0), "row")
        lower_f = jnp.linalg.cholesky(diagonal)
        inverse = jax.scipy.linalg.solve_triangular(lower_f, identity, lower=True)
        panel_cols = dot_high(strip_cols, inverse)
        panel_cols = jnp.where((row_tiles >= 2 * panel_no)[:, None], panel_cols, 0.0)
        columns.append(panel_cols)
        trail_rows = jnp.where((row_tiles >= 2 * panel_no + 2)[:, None], panel_cols, 0.0)
        picked = lax.dynamic_index_in_dim(
            trail_rows.reshape(local_ct, ratio, TILE, PANEL), offset, 1, keepdims=False
        )
        picked = picked.reshape(local_ct * TILE, PANEL)
        trail_cols = broadcast(picked.astype(jnp.bfloat16), "row", col_id % row_count).astype(
            picked.dtype
        )
        front_mat = front_mat - dot_high(trail_rows, trail_cols)
    return (front_mat[None], jnp.concatenate(columns, axis=1)[None])


def solution(mesh):
    placed = (P("front", "row", "col"), P(("front", "row"), "col"), P())
    return jax.shard_map(
        per_device,
        mesh=mesh,
        in_specs=placed,
        out_specs=(P("front", "row", "col"), P("front", "row", None)),
        check_vma=False,
    )
```

profile of v0, /device:TPU:32, one launch (start us, length us, event | category | flops | bytes accessed | tf_op | source)
XLA Modules:
  0.0 993.1 jit_solution(12782140775272528399)
XLA Ops:
  9.4 2.2 copy.33
  12.5 3.1 broadcast_in_dim.113
  15.6 8.6 scatter_fusion
  24.2 15.5 %all-to-all-start = ((bf16[128,128,128]{2,1,0:T(8,128)(2,1)}), bf16[128,128,128]{2,1,0:T(8,128)(2,1)}, u32[]{:S(2)}, u32[]{:S(2)}) async-start(bf16[128,128,128]{2,1,0:T(8,128)(2,1)} %scatter_fusion), calls=%async_computation | async-start | bytes 8388608 | tf_op jit(solution)/shard_map/all_to_all | solution.py:71
  40.1 4.8 gather_fusion
  45.2 1.5 gather_fusion.1
  48.2 4.8 convert_element_type.26
  53.0 2.1 copy.19
  55.1 82.4 %all-to-all-done = bf16[128,128,128]{2,1,0:T(8,128)(2,1)} async-done(((bf16[128,128,128]{2,1,0:T(8,128)(2,1)}), bf16[128,128,128]{2,1,0:T(8,128)(2,1)}, u32[]{:S(2)}, u32[]{:S(2)}) %all-to-all-start) | async-done | bytes 4194336 | tf_op jit(solution)/shard_map/all_to_all | solution.py:71
  137.5 5.0 dynamic-slice_bitcast_fusion.1
  142.5 0.7 collective-permute-start
  143.2 31.0 %scatter_custom_fusion = s32[128]{0:T(128)S(1)} fusion(s32[8192]{0:T(1024)S(1)} %bitcast.145, s32[8192]{0:T(1024)S(1)} %reshape.847, s32[]{:T(128)} %constant.303.clone.1), kind=kCustom, calls=%fused_computation.185 | custom fusion | bytes 516 | tf_op jit(solution)/shard_map/scatter | solution.py:100
  174.2 2.8 pad_convert_fusion
  177.0 12.9 %collective-permute-done = bf16[8,8,1,128,128]{4,3,1,0,2:T(8,128)(2,1)} collective-permute-done((bf16[8,8,1,128,128]{4,3,1,0,2:T(8,128)(2,1)}, bf16[8,8,1,128,128]{4,3,1,0,2:T(8,128)(2,1)}, u32[]{:S(2)}, u32[]{:S(2)}) %collective-permute-start) | collective-permute-done | bytes 2097184 | tf_op jit(solution)/shard_map/ppermute | solution.py:20
  189.9 2.0 pad_maximum_fusion
  191.9 4.6 bitcast_convert_fusion
  196.5 25.6 %scatter_fusion.1 = f32[73,128,128]{2,1,0:T(8,128)} fusion(f32[73,128,128]{2,1,0:T(8,128)} %pad_convert_fusion, s32[128]{0:T(128)S(1)} %compare_select_fusion.6, f32[128,128,128]{2,1,0:T(8,128)} %bitcast_convert_fusion), kind=kCustom, calls=%fused_computation.6 | custom fusion | flops 2097152 | bytes 25166336 | tf_op jit(solution)/shard_map/scatter-add | solution.py:110
  222.1 5.1 slice.82
  227.2 6.6 copy.31
  233.8 5.1 copy.36
  238.9 2.2 copy-done.2
  241.1 1.4 slice_select_fusion.2
  242.6 106.2 %all-reduce.21.cloned.1.call-done = (f32[1536,128]{0,1:T(8,128)}, f32[1536,128]{0,1:T(8,128)}) async-done(((f32[1536,128]{0,1:T(8,128)}, f32[1536,128]{0,1:T(8,128)}), (f32[1536,128]{0,1:T(8,128)}, f32[1536,128]{0,1:T(8,128)})) %all-reduce.21.cloned.1.call-update) | async-done | bytes 1572880 | tf_op jit(solution)/shard_map/psum | solution.py:25
  348.8 1.3 constant_dynamic-update-slice_fusion.1
  350.2 1.1 copy-done.6
  351.4 0.7 pad_maximum_fusion.1
  352.5 92.4 %all-reduce.11.cloned.1.call-done = f32[256,256]{0,1:T(8,128)} async-done(((f32[256,256]{0,1:T(8,128)}), f32[256,256]{0,1:T(8,128)}) %all-reduce.11.cloned.1.call-update) | async-done | bytes 262160 | tf_op jit(solution)/shard_map/psum | solution.py:133
  444.9 1.1 copy.23
  445.9 1.0 fusion.9
  447.0 11.7 %cholesky.130 = f32[128,128]{1,0:T(8,128)S(1)} custom-call(f32[128,128]{1,0:T(8,128)S(1)} %cholesky.194), custom_call_target="Cholesky" | custom-call | tf_op jit(solution)/shard_map/jit(cholesky)/cholesky | solution.py:134
  458.7 9.8 custom-call.17
  469.0 11.7 %cholesky.147 = f32[128,128]{1,0:T(8,128)S(1)} custom-call(f32[128,128]{1,0:T(8,128)S(1)} %convolution_subtract_fusion.4), custom_call_target="Cholesky" | custom-call | tf_op jit(solution)/shard_map/jit(cholesky)/cholesky | solution.py:134
  480.8 0.7 compare_reduce_fusion.2
  483.5 4.1 while.4
  484.3 1.3 bitcast_dynamic-update-slice_fusion.4
  486.2 1.3 bitcast_dynamic-update-slice_fusion.4
  487.6 19.7 %custom-call.18 = f32[2,128,128]{1,2,0:T(8,128)S(1)} custom-call(f32[2,128,128]{2,1,0:T(8,128)S(1)} %get-tuple-element.18), custom_call_target="InvertDiagBlocksLowerTriangular" | custom-call | tf_op jit(solution)/shard_map/jit(_solve_triangular)/triangular_solve | solution.py:135
  508.2 4.6 broadcast_select_fusion.1
  512.8 0.8 fusion
  513.7 88.3 %all-reduce.13.cloned.1.call-done = bf16[768,256]{1,0:T(8,128)(2,1)} async-done(((bf16[768,256]{1,0:T(8,128)(2,1)}), bf16[768,256]{1,0:T(8,128)(2,1)}) %all-reduce.13.cloned.1.call-update) | async-done | bytes 393232 | tf_op jit(solution)/shard_map/psum | solution.py:25
  602.0 4.9 convolution_subtract_fusion
  606.9 2.2 copy-done.3
  609.0 1.3 slice_select_fusion
  610.5 108.9 %all-reduce.19.cloned.1.call-done = (f32[1536,128]{0,1:T(8,128)}, f32[1536,128]{0,1:T(8,128)}) async-done(((f32[1536,128]{0,1:T(8,128)}, f32[1536,128]{0,1:T(8,128)}), (f32[1536,128]{0,1:T(8,128)}, f32[1536,128]{0,1:T(8,128)})) %all-reduce.19.cloned.1.call-update) | async-done | bytes 1572880 | tf_op jit(solution)/shard_map/psum | solution.py:25
  719.3 1.3 constant_dynamic-update-slice_fusion.3
  720.7 1.1 copy-done.7
  721.9 0.7 pad_maximum_fusion.2
  723.2 92.2 %all-reduce.15.cloned.1.call-done = f32[256,256]{0,1:T(8,128)} async-done(((f32[256,256]{0,1:T(8,128)}), f32[256,256]{0,1:T(8,128)}) %all-reduce.15.cloned.1.call-update) | async-done | bytes 262160 | tf_op jit(solution)/shard_map/psum | solution.py:133
  815.4 1.1 copy.26
  816.4 1.0 fusion.8
  817.5 11.7 %cholesky.164 = f32[128,128]{1,0:T(8,128)S(1)} custom-call(f32[128,128]{1,0:T(8,128)S(1)} %cholesky.197), custom_call_target="Cholesky" | custom-call | tf_op jit(solution)/shard_map/jit(cholesky)/cholesky | solution.py:134
  829.2 9.8 custom-call.19
  839.5 11.7 %cholesky.181 = f32[128,128]{1,0:T(8,128)S(1)} custom-call(f32[128,128]{1,0:T(8,128)S(1)} %convolution_subtract_fusion.3), custom_call_target="Cholesky" | custom-call | tf_op jit(solution)/shard_map/jit(cholesky)/cholesky | solution.py:134
  851.3 0.7 compare_reduce_fusion
  853.9 4.1 while.5
  854.7 1.3 bitcast_dynamic-update-slice_fusion.5
  856.6 1.3 bitcast_dynamic-update-slice_fusion.5
  858.0 19.7 %custom-call.20 = f32[2,128,128]{1,2,0:T(8,128)S(1)} custom-call(f32[2,128,128]{2,1,0:T(8,128)S(1)} %get-tuple-element.19), custom_call_target="InvertDiagBlocksLowerTriangular" | custom-call | tf_op jit(solution)/shard_map/jit(_solve_triangular)/triangular_solve | solution.py:135
  878.6 5.6 broadcast_select_fusion
  884.1 0.8 fusion.1
  884.9 3.5 maximum_bitcast_fusion
  888.4 84.8 %all-reduce.17.cloned.1.call-done = bf16[768,256]{1,0:T(8,128)(2,1)} async-done(((bf16[768,256]{1,0:T(8,128)(2,1)}), bf16[768,256]{1,0:T(8,128)(2,1)}) %all-reduce.17.cloned.1.call-update) | async-done | bytes 393232 | tf_op jit(solution)/shard_map/psum | solution.py:25
  973.2 6.7 subtract_bitcast_fusion
  980.0 6.1 copy.28
  (117 shorter events, 13.4 us)
Async XLA Ops:
  7.2 0.7 copy-start
  24.2 113.3 %all-to-all-start = ((bf16[128,128,128]{2,1,0:T(8,128)(2,1)}), bf16[128,128,128]{2,1,0:T(8,128)(2,1)}, u32[]{:S(2)}, u32[]{:S(2)}) async-start(bf16[128,128,128]{2,1,0:T(8,128)(2,1)} %scatter_fusion), calls=%async_computation | async-start | bytes 8388608 | tf_op jit(solution)/shard_map/all_to_all | solution.py:71
  39.6 309.2 %all-reduce.21.cloned.1.call-start = ((), (), s32[]{:S(2)}) async-start(), calls=%async_computation.6 | async-start | bytes 3145728 | tf_op jit(solution)/shard_map/psum | solution.py:25
  137.5 36.7 %copy-start.4 = (bf16[12,6,128,128]{3,2,1,0:T(8,128)(2,1)S(1)}, bf16[12,6,128,128]{3,2,1,0:T(8,128)(2,1)}, u32[]{:S(2)}) copy-start(bf16[12,6,128,128]{3,2,1,0:T(8,128)(2,1)} %copy.19) | copy-start | bytes 7077892
  142.5 47.5 %collective-permute-start = (bf16[8,8,1,128,128]{4,3,1,0,2:T(8,128)(2,1)}, bf16[8,8,1,128,128]{4,3,1,0,2:T(8,128)(2,1)}, u32[]{:S(2)}, u32[]{:S(2)}) collective-permute-start(bf16[8,8,1,128,128]{4,3,1,0,2:T(8,128)(2,1)} %get-tuple-element.55), channel_id=1, source_target_pairs={{0,128},{128,0},{1,129},{129,1},{2,130},{130,2},{3,131},{131,3},{4... | collective-permute-start | bytes 6291464 | tf_op jit(solution)/shard_map/ppermute | solution.py:20
  174.2 15.8 %copy-start.5 = (bf16[1,8,8,1,128,128]{5,4,2,1,0,3:T(8,128)(2,1)S(1)}, bf16[1,8,8,1,128,128]{5,4,2,1,0,3:T(8,128)(2,1)}, u32[]{:S(2)}) copy-start(bf16[1,8,8,1,128,128]{5,4,2,1,0,3:T(8,128)(2,1)} %get-tuple-element.54) | copy-start | bytes 6291460
  238.9 2.2 copy-start.2
  242.4 202.4 %all-reduce.11.cloned.1.call-start = ((), (), s32[]{:S(2)}) async-start(), calls=%async_computation.1 | async-start | bytes 524288 | tf_op jit(solution)/shard_map/psum | solution.py:133
  348.8 1.4 copy-start.8
  350.2 1.1 copy-start.6
  352.1 249.9 %all-reduce.13.cloned.1.call-start = ((), (), s32[]{:S(2)}) async-start(), calls=%async_computation.2 | async-start | bytes 786432 | tf_op jit(solution)/shard_map/psum | solution.py:25
  513.6 205.7 %all-reduce.19.cloned.1.call-start = ((), (), s32[]{:S(2)}) async-start(), calls=%async_computation.5 | async-start | bytes 3145728 | tf_op jit(solution)/shard_map/psum | solution.py:25
  606.9 2.2 copy-start.3
  610.4 205.0 %all-reduce.15.cloned.1.call-start = ((), (), s32[]{:S(2)}) async-start(), calls=%async_computation.3 | async-start | bytes 524288 | tf_op jit(solution)/shard_map/psum | solution.py:133
  719.3 1.4 copy-start.9
  720.7 1.1 copy-start.7
  722.6 250.6 %all-reduce.17.cloned.1.call-start = ((), (), s32[]{:S(2)}) async-start(), calls=%async_computation.4 | async-start | bytes 786432 | tf_op jit(solution)/shard_map/psum | solution.py:25
  980.0 6.1 copy-start.1
Sparse Core Ops, SparseCore 0:
  242.6 106.2 all-reduce.20
  352.3 92.5 all-reduce.10
  513.8 88.1 all-reduce.12
  610.5 108.7 all-reduce.18
  722.8 92.5 all-reduce.14
  885.1 88.1 all-reduce.16
where the time goes:
time: 1000 us; the launch traced here: 993 us
  waiting for transfers between devices  668 us (67%)
  other arithmetic  156 us (16%)
  local copies, waits for them, and re-layouts  109 us (11%)
  matrix products  24.5 us (2%)
  between operations  17.5 us (2%)
  starting transfers between devices  17 us (2%)
    psum x4, waiting for transfers between devices, broadcast(): return lax.psum(block, axis)  388 us
    psum x2, waiting for transfers between devices, per_device(): diagonal = lax.psum(jnp.concatenate(block_rows, axis=0), 'row')  185 us
    all_to_all x1, waiting for transfers between devices, per_device(): lax.all_to_all(outgoing, ('row', 'col'), split_axis=0, concat_axis=0, til...  82.4 us
    another operation x14, other arithmetic, per_device(): lower_f = jnp.linalg.cholesky(diagonal)  69.3 us
    another operation x5, other arithmetic, per_device(): inverse = jax.scipy.linalg.solve_triangular(lower_f, identity, lower=True)  39.4 us
    scatter x1, local copies, waits for them, and re-layouts, per_device(): slot_table = jnp.full((slot_count,), spare_tile, jnp.int32).at[position.r...  31 us
    scatter-add x1, other arithmetic, per_device(): tile_sums = tile_sums.at[slot_table].add(received.astype(jnp.float32))  25.6 us
    unnamed x25, local copies, waits for them, and re-layouts  23.3 us
  transfers between devices with their start and end apart: 8, of which 8 were waited for; matrix products, arithmetic and copies ran while one was open for 5% of the time, Pallas kernels for 0%

commit v1 on v0

--- a/solution.py
+++ b/solution.py
@@ -130,7 +130,7 @@
             local_no = tile_no // row_count
             rows_here = strip_cols[local_no * TILE : (local_no + 1) * TILE]
             block_rows.append(jnp.where(row_id == tile_no % row_count, rows_here, 0.0))
-        diagonal = lax.psum(jnp.concatenate(block_rows, axis=0), "row")
+        diagonal = jnp.sum(lax.all_gather(jnp.concatenate(block_rows, axis=0), "row"), axis=0)
         lower_f = jnp.linalg.cholesky(diagonal)
         inverse = jax.scipy.linalg.solve_triangular(lower_f, identity, lower=True)
         panel_cols = dot_high(strip_cols, inverse)

time: 1000 us -> 925 us (0.925)
  waiting for transfers between devices: 668 us -> 611 us
  local copies, waits for them, and re-layouts: 109 us -> 91.5 us
    psum x2 -> x0, waiting for transfers between devices: 185 us -> none  [per_device(): diagonal = lax.psum(jnp.concatenate(block_rows, axis=0), 'row')]
    all_gather x0 -> x2, waiting for transfers between devices: none -> 126 us  [per_device(): lax.all_gather(jnp.concatenate(block_rows, axis=0), 'row')]
    unnamed x25 -> x24, local copies, waits for them, and re-layouts: 23.3 us -> 13.3 us
  transfers between devices with their start and end apart: 8 -> 8, of which waited for: 8 -> 8; matrix products, arithmetic and copies ran while one was open for 5% -> 6% of each run, Pallas kernels for 0% -> 0%
where the time goes in v1:
time: 925 us; the launch traced here: 917 us
  waiting for transfers between devices  611 us (66%)
  other arithmetic  158 us (17%)
  local copies, waits for them, and re-layouts  91.5 us (10%)
  matrix products  21.5 us (2%)
  between operations  17.9 us (2%)
  starting transfers between devices  16.8 us (2%)
    psum x4, waiting for transfers between devices, broadcast(): return lax.psum(block, axis)  390 us
    all_gather x2, waiting for transfers between devices, per_device(): lax.all_gather(jnp.concatenate(block_rows, axis=0), 'row')  126 us
    all_to_all x1, waiting for transfers between devices, per_device(): lax.all_to_all(outgoing, ('row', 'col'), split_axis=0, concat_axis=0, til...  82.4 us
    another operation x14, other arithmetic, per_device(): lower_f = jnp.linalg.cholesky(diagonal)  69.3 us
    another operation x5, other arithmetic, per_device(): inverse = jax.scipy.linalg.solve_triangular(lower_f, identity, lower=True)  39.4 us
    scatter x1, local copies, waits for them, and re-layouts, per_device(): slot_table = jnp.full((slot_count,), spare_tile, jnp.int32).at[position.r...  31 us
    scatter-add x1, other arithmetic, per_device(): tile_sums = tile_sums.at[slot_table].add(received.astype(jnp.float32))  25.6 us
    dot_general x4, matrix products, dot_high(): lax.dot_general(left_mat, right_mat, (((1,), (1,)), ((), ())), precision=...  18.8 us
  transfers between devices with their start and end apart: 8, of which 8 were waited for; matrix products, arithmetic and copies ran while one was open for 6% of the time, Pallas kernels for 0%

profile of v1, /device:TPU:32, one launch (start us, length us, event | category | flops | bytes accessed | tf_op | source)
XLA Modules:
  0.0 916.7 jit_solution(17198526406312894313)
XLA Ops:
  7.9 0.7 gather_fusion.3
  8.6 0.6 gather_fusion.2
  9.4 2.2 copy.21
  12.5 3.1 broadcast_in_dim.113
  15.6 8.6 scatter_fusion
  24.2 15.5 %all-to-all-start = ((bf16[128,128,128]{2,1,0:T(8,128)(2,1)}), bf16[128,128,128]{2,1,0:T(8,128)(2,1)}, u32[]{:S(2)}, u32[]{:S(2)}) async-start(bf16[128,128,128]{2,1,0:T(8,128)(2,1)} %scatter_fusion), calls=%async_computation | async-start | bytes 8388608 | tf_op jit(solution)/shard_map/all_to_all | solution.py:71
  40.1 4.8 gather_fusion
  45.2 1.5 gather_fusion.1
  48.2 4.8 convert_element_type.26
  53.0 2.1 copy.16
  55.1 82.4 %all-to-all-done = bf16[128,128,128]{2,1,0:T(8,128)(2,1)} async-done(((bf16[128,128,128]{2,1,0:T(8,128)(2,1)}), bf16[128,128,128]{2,1,0:T(8,128)(2,1)}, u32[]{:S(2)}, u32[]{:S(2)}) %all-to-all-start) | async-done | bytes 4194336 | tf_op jit(solution)/shard_map/all_to_all | solution.py:71
  137.5 5.0 dynamic-slice_bitcast_fusion.1
  142.5 0.7 collective-permute-start
  143.2 31.0 %scatter_custom_fusion = s32[128]{0:T(128)S(1)} fusion(s32[8192]{0:T(1024)S(1)} %bitcast.147, s32[8192]{0:T(1024)S(1)} %reshape.847, s32[]{:T(128)} %constant.303.clone.1), kind=kCustom, calls=%fused_computation.185 | custom fusion | bytes 516 | tf_op jit(solution)/shard_map/scatter | solution.py:100
  174.2 2.8 pad_convert_fusion
  177.0 12.9 %collective-permute-done = bf16[8,8,1,128,128]{4,3,1,0,2:T(8,128)(2,1)} collective-permute-done((bf16[8,8,1,128,128]{4,3,1,0,2:T(8,128)(2,1)}, bf16[8,8,1,128,128]{4,3,1,0,2:T(8,128)(2,1)}, u32[]{:S(2)}, u32[]{:S(2)}) %collective-permute-start) | collective-permute-done | bytes 2097184 | tf_op jit(solution)/shard_map/ppermute | solution.py:20
  189.9 2.0 pad_maximum_fusion
  191.9 4.6 bitcast_convert_fusion
  196.5 25.6 %scatter_fusion.1 = f32[73,128,128]{2,1,0:T(8,128)} fusion(f32[73,128,128]{2,1,0:T(8,128)} %pad_convert_fusion, s32[128]{0:T(128)S(1)} %compare_select_fusion.6, f32[128,128,128]{2,1,0:T(8,128)} %bitcast_convert_fusion), kind=kCustom, calls=%fused_computation.6 | custom fusion | flops 2097152 | bytes 25166336 | tf_op jit(solution)/shard_map/scatter-add | solution.py:110
  222.1 2.9 slice.82
  225.0 2.9 copy.18
  227.9 1.2 copy.24
  229.1 2.2 copy-done.2
  231.3 1.2 slice_select_fusion.2
  232.6 106.3 %all-reduce.15.cloned.1.call-done = (f32[1536,128]{1,0:T(8,128)}, f32[1536,128]{1,0:T(8,128)}) async-done(((f32[1536,128]{1,0:T(8,128)}, f32[1536,128]{1,0:T(8,128)}), (f32[1536,128]{1,0:T(8,128)}, f32[1536,128]{1,0:T(8,128)})) %all-reduce.15.cloned.1.call-update) | async-done | bytes 1572880 | tf_op jit(solution)/shard_map/psum | solution.py:25
  338.9 1.3 constant_dynamic-update-slice_fusion.1
  340.4 1.1 copy-done.6
  341.5 0.7 pad_maximum_fusion.1
  342.7 62.7 %all-gather.5.cloned.1.call-done = f32[2048,256]{1,0:T(8,128)} async-done(((f32[256,256]{1,0:T(8,128)}), f32[2048,256]{1,0:T(8,128)}) %all-gather.5.cloned.1.call-update) | async-done | bytes 2097168 | tf_op jit(solution)/shard_map/all_gather | solution.py:133
  405.5 1.8 reduce_sum.18
  407.4 11.7 %cholesky.130 = f32[128,128]{1,0:T(8,128)S(1)} custom-call(f32[128,128]{1,0:T(8,128)S(1)} %cholesky.194), custom_call_target="Cholesky" | custom-call | tf_op jit(solution)/shard_map/jit(cholesky)/cholesky | solution.py:134
  419.2 9.8 %custom-call.17 = f32[1,128,128]{1,2,0:T(8,128)S(1)} custom-call(f32[1,128,128]{2,1,0:T(8,128)S(1)} %get-tuple-element.61), custom_call_target="InvertDiagBlocksLowerTriangular" | custom-call | tf_op jit(solution)/shard_map/jit(cholesky)/cholesky | solution.py:134
  429.5 11.7 %cholesky.147 = f32[128,128]{1,0:T(8,128)S(1)} custom-call(f32[128,128]{1,0:T(8,128)S(1)} %convolution_subtract_fusion.4), custom_call_target="Cholesky" | custom-call | tf_op jit(solution)/shard_map/jit(cholesky)/cholesky | solution.py:134
  441.2 0.7 compare_reduce_fusion.2
  442.0 0.6 compare_reduce_fusion.3
  443.9 4.1 while.4
  444.8 1.3 bitcast_dynamic-update-slice_fusion.4
  446.7 1.3 bitcast_dynamic-update-slice_fusion.4
  448.1 19.7 %custom-call.18 = f32[2,128,128]{1,2,0:T(8,128)S(1)} custom-call(f32[2,128,128]{2,1,0:T(8,128)S(1)} %get-tuple-element.18), custom_call_target="InvertDiagBlocksLowerTriangular" | custom-call | tf_op jit(solution)/shard_map/jit(_solve_triangular)/triangular_solve | solution.py:135
  468.6 3.1 broadcast_select_fusion.1
  471.8 0.8 fusion
  472.7 89.0 %all-reduce.9.cloned.1.call-done = bf16[768,256]{1,0:T(8,128)(2,1)} async-done(((bf16[768,256]{1,0:T(8,128)(2,1)}), bf16[768,256]{1,0:T(8,128)(2,1)}) %all-reduce.9.cloned.1.call-update) | async-done | bytes 393232 | tf_op jit(solution)/shard_map/psum | solution.py:25
  561.7 4.8 convolution_subtract_fusion
  566.5 2.2 copy-done.3
  568.7 1.2 slice_select_fusion
  570.0 108.9 %all-reduce.13.cloned.1.call-done = (f32[1536,128]{1,0:T(8,128)}, f32[1536,128]{1,0:T(8,128)}) async-done(((f32[1536,128]{1,0:T(8,128)}, f32[1536,128]{1,0:T(8,128)}), (f32[1536,128]{1,0:T(8,128)}, f32[1536,128]{1,0:T(8,128)})) %all-reduce.13.cloned.1.call-update) | async-done | bytes 1572880 | tf_op jit(solution)/shard_map/psum | solution.py:25
  678.9 1.3 constant_dynamic-update-slice_fusion.3
  680.3 1.1 copy-done.7
  681.5 0.7 pad_maximum_fusion.2
  682.6 62.8 %all-gather.7.cloned.1.call-done = f32[2048,256]{1,0:T(8,128)} async-done(((f32[256,256]{1,0:T(8,128)}), f32[2048,256]{1,0:T(8,128)}) %all-gather.7.cloned.1.call-update) | async-done | bytes 2097168 | tf_op jit(solution)/shard_map/all_gather | solution.py:133
  745.4 1.8 reduce_sum.19
  747.4 11.7 %cholesky.164 = f32[128,128]{1,0:T(8,128)S(1)} custom-call(f32[128,128]{1,0:T(8,128)S(1)} %cholesky.197), custom_call_target="Cholesky" | custom-call | tf_op jit(solution)/shard_map/jit(cholesky)/cholesky | solution.py:134
  759.2 9.8 %custom-call.19 = f32[1,128,128]{1,2,0:T(8,128)S(1)} custom-call(f32[1,128,128]{2,1,0:T(8,128)S(1)} %get-tuple-element.57), custom_call_target="InvertDiagBlocksLowerTriangular" | custom-call | tf_op jit(solution)/shard_map/jit(cholesky)/cholesky | solution.py:134
  769.4 11.7 %cholesky.181 = f32[128,128]{1,0:T(8,128)S(1)} custom-call(f32[128,128]{1,0:T(8,128)S(1)} %convolution_subtract_fusion.3), custom_call_target="Cholesky" | custom-call | tf_op jit(solution)/shard_map/jit(cholesky)/cholesky | solution.py:134
  781.2 0.7 compare_reduce_fusion
  783.8 4.2 while.5
  784.7 1.3 bitcast_dynamic-update-slice_fusion.5
  786.7 1.3 bitcast_dynamic-update-slice_fusion.5
  788.0 19.7 %custom-call.20 = f32[2,128,128]{1,2,0:T(8,128)S(1)} custom-call(f32[2,128,128]{2,1,0:T(8,128)S(1)} %get-tuple-element.19), custom_call_target="InvertDiagBlocksLowerTriangular" | custom-call | tf_op jit(solution)/shard_map/jit(_solve_triangular)/triangular_solve | solution.py:135
  808.6 4.0 broadcast_select_fusion
  812.7 0.8 fusion.1
  813.5 3.5 maximum_bitcast_fusion
  817.0 85.6 %all-reduce.11.cloned.1.call-done = bf16[768,256]{1,0:T(8,128)(2,1)} async-done(((bf16[768,256]{1,0:T(8,128)(2,1)}), bf16[768,256]{1,0:T(8,128)(2,1)}) %all-reduce.11.cloned.1.call-update) | async-done | bytes 393232 | tf_op jit(solution)/shard_map/psum | solution.py:25
  902.6 6.8 subtract_bitcast_fusion
  (118 shorter events, 11.6 us)
Async XLA Ops:
  7.2 0.7 copy-start
  24.2 113.3 %all-to-all-start = ((bf16[128,128,128]{2,1,0:T(8,128)(2,1)}), bf16[128,128,128]{2,1,0:T(8,128)(2,1)}, u32[]{:S(2)}, u32[]{:S(2)}) async-start(bf16[128,128,128]{2,1,0:T(8,128)(2,1)} %scatter_fusion), calls=%async_computation | async-start | bytes 8388608 | tf_op jit(solution)/shard_map/all_to_all | solution.py:71
  39.6 299.3 %all-reduce.15.cloned.1.call-start = ((), (), s32[]{:S(2)}) async-start(), calls=%async_computation.6 | async-start | bytes 3145728 | tf_op jit(solution)/shard_map/psum | solution.py:25
  137.5 36.7 %copy-start.4 = (bf16[12,6,128,128]{3,2,1,0:T(8,128)(2,1)S(1)}, bf16[12,6,128,128]{3,2,1,0:T(8,128)(2,1)}, u32[]{:S(2)}) copy-start(bf16[12,6,128,128]{3,2,1,0:T(8,128)(2,1)} %copy.16) | copy-start | bytes 7077892
  142.5 47.5 %collective-permute-start = (bf16[8,8,1,128,128]{4,3,1,0,2:T(8,128)(2,1)}, bf16[8,8,1,128,128]{4,3,1,0,2:T(8,128)(2,1)}, u32[]{:S(2)}, u32[]{:S(2)}) collective-permute-start(bf16[8,8,1,128,128]{4,3,1,0,2:T(8,128)(2,1)} %get-tuple-element.49), channel_id=1, source_target_pairs={{0,128},{128,0},{1,129},{129,1},{2,130},{130,2},{3,131},{131,3},{4... | collective-permute-start | bytes 6291464 | tf_op jit(solution)/shard_map/ppermute | solution.py:20
  174.2 15.8 %copy-start.5 = (bf16[1,8,8,1,128,128]{5,4,2,1,0,3:T(8,128)(2,1)S(1)}, bf16[1,8,8,1,128,128]{5,4,2,1,0,3:T(8,128)(2,1)}, u32[]{:S(2)}) copy-start(bf16[1,8,8,1,128,128]{5,4,2,1,0,3:T(8,128)(2,1)} %get-tuple-element.48) | copy-start | bytes 6291460
  229.1 2.2 copy-start.2
  232.6 172.9 %all-gather.5.cloned.1.call-start = ((), (), s32[]{:S(2)}) async-start(), calls=%async_computation.3 | async-start | bytes 2359296 | tf_op jit(solution)/shard_map/all_gather | solution.py:133
  338.9 1.4 copy-start.9
  340.4 1.1 copy-start.6
  342.3 219.4 %all-reduce.9.cloned.1.call-start = ((), (), s32[]{:S(2)}) async-start(), calls=%async_computation.1 | async-start | bytes 786432 | tf_op jit(solution)/shard_map/psum | solution.py:25
  472.6 206.3 %all-reduce.13.cloned.1.call-start = ((), (), s32[]{:S(2)}) async-start(), calls=%async_computation.5 | async-start | bytes 3145728 | tf_op jit(solution)/shard_map/psum | solution.py:25
  566.5 2.2 copy-start.3
  569.9 175.5 %all-gather.7.cloned.1.call-start = ((), (), s32[]{:S(2)}) async-start(), calls=%async_computation.4 | async-start | bytes 2359296 | tf_op jit(solution)/shard_map/all_gather | solution.py:133
  678.9 1.4 copy-start.8
  680.3 1.1 copy-start.7
  682.2 220.4 %all-reduce.11.cloned.1.call-start = ((), (), s32[]{:S(2)}) async-start(), calls=%async_computation.2 | async-start | bytes 786432 | tf_op jit(solution)/shard_map/psum | solution.py:25
  902.6 6.8 copy-start.1
Sparse Core Ops, SparseCore 0:
  232.7 106.2 all-reduce.14
  342.4 63.0 all-gather.4
  472.7 88.8 all-reduce.8
  570.1 108.7 all-reduce.12
  682.3 63.0 all-gather.6
  813.6 88.9 all-reduce.10
